TPU v7x, 32 devices: a whole 2x2x4 slice. The times are simulated.
32 devices in a mesh: xline: 4 (over y, x), inline: 8 (over z, core).
Axes of the slice: x: 2, y: 2, z: 4, core: 2. Of those that a mesh axis runs over, the one named last changes fastest.
Arguments:
- pressure: float32 [256, 256, 256], P('inline', 'xline'), may hold values from -6 to 6
- vel_inline: float32 [256, 256, 256], P('inline', 'xline'), may hold values from -6 to 6
- vel_xline: float32 [256, 256, 256], P('inline', 'xline'), may hold values from -6 to 6
- vel_depth: float32 [256, 256, 256], P('inline', 'xline'), may hold values from -6 to 6
- modulus: float32 [256, 256, 256], P('inline', 'xline'), may hold values from 0.5 to 1.5
- buoyancy: float32 [256, 256, 256], P('inline', 'xline'), may hold values from 0.5 to 1.5
- traces: float32 [24576, 512], P(('xline', 'inline')), may hold values from -6 to 6
- owner: int32 [24576, 1], P(('xline', 'inline')), may hold values from 0 to 31; in each aligned block of 768 rows (0 to 767, 768 to 1535, ...) at most 60 rows name the same one
- node_cell: int32 [24576], P(('xline', 'inline')), may hold values from 0 to 524287
- resample: float32 [4, 512], replicated, may hold values from -0.25 to 0.25
Outputs:
- pressure_out: float32 [256, 256, 256], P('inline', 'xline')
- inline_out: float32 [256, 256, 256], P('inline', 'xline')
- xline_out: float32 [256, 256, 256], P('inline', 'xline')
- depth_out: float32 [256, 256, 256], P('inline', 'xline')
Inputs may be any that keep to these rules, and one draw needn't show every extreme that they name: Among the nodes of one device, at most 60 have the same owner.
All inputs are finite; a program needn't handle non-finite values.
Results may differ from a plain program's by a relative error of at most 0.0002.
Values sent between devices are 32-bit elements; how exact they have to be, the bound alone decides.
No kernel may reach another device: no remote copies, remote signals or barrier semaphores. Data moves between devices by JAX's collectives and lax.ppermute only.
A program may use at most 128 MiB of HBM per device.

v0:
```python
import functools

import jax
import jax.numpy as jnp
from jax import lax
from jax.experimental import pallas as pl
from jax.experimental.pallas import tpu as pltpu
from jax.sharding import PartitionSpec as P

STEPS = 4
COURANT = 0.35
HALO = 4
REACH = 3
SLOTS = 128
VMEM_LIMIT = 64 * 1024 * 1024
BATCH = 8
PARTS = SLOTS // BATCH
PART_BITS = PARTS.bit_length() - 1
UNROLL = 4
GROUPS = 8
FLAG = 4096.0
F32 = jnp.float32
BF16 = jnp.bfloat16
ANY = pl.BlockSpec(memory_space=pl.ANY)
VMEM = pl.BlockSpec(memory_space=pltpu.VMEM)
SMEM = pl.BlockSpec(memory_space=pltpu.SMEM)


def rotate(value, axis, steps):
    count = lax.axis_size(axis)
    return lax.ppermute(value, axis, [(source, (source + steps) % count) for source in range(count)])


def iota(shape, dim):
    return lax.broadcasted_iota(jnp.int32, shape, dim)


def lane_before(value):
    lanes = value.ndim - 1
    return jnp.where(iota(value.shape, lanes) == 0, 0.0, pltpu.roll(value, 1, lanes))


def lane_after(value):
    lanes = value.ndim - 1
    width = value.shape[lanes]
    return jnp.where(iota(value.shape, lanes) == width - 1, 0.0, pltpu.roll(value, width - 1, lanes))


def row_before(value):
    return jnp.where(iota(value.shape, 0) == 0, 0.0, pltpu.roll(value, 1, 0))


def half_turn(tile):
    return pltpu.roll(tile, 4, 0)


def run_copies(copies):
    for copy in copies:
        copy.start()
    return copies


class Either:
    def __init__(self, choice, first, second, index, target, sem):
        self.choice = choice
        sources = [ref.at[index] if index != () else ref for ref in (first, second)]
        self.copies = [pltpu.make_async_copy(ref, target, sem) for ref in sources]

    def start(self):
        pl.when(self.choice)(self.copies[0].start)
        pl.when(jnp.logical_not(self.choice))(self.copies[1].start)

    def wait(self):
        self.copies[0].wait()


def edge_pack_kernel(
    p, vi, vx, vd, m, b, low_out, high_out, near_out, far_out,
    strips, low, high, down, up, vel, col_sems, sems, out_sems,
):
    planes, columns, depth = p.shape
    col_copies = []
    for side, start in ((0, 0), (1, columns - 8)):
        for field, ref in enumerate((vi, vx, vd, p, m, b)):
            col_copies.append(
                pltpu.make_async_copy(
                    ref.at[:, pl.ds(start, 8), :], strips.at[side, field], col_sems.at[side, field]
                )
            )
    jobs = (
        (vi, 0, 3, vel.at[0, pl.ds(1, 3)]),
        (vx, 0, 3, vel.at[1, pl.ds(1, 3)]),
        (vd, 0, 3, vel.at[2, pl.ds(1, 3)]),
        (vi, planes - 4, 4, vel.at[3]),
        (vx, planes - 4, 4, vel.at[4]),
        (vd, planes - 4, 4, vel.at[5]),
        (p, 0, 4, down.at[pl.ds(0, 4)]),
        (m, 0, 3, down.at[pl.ds(7, 3)]),
        (b, 0, 3, down.at[pl.ds(10, 3)]),
        (p, planes - 4, 4, up.at[pl.ds(0, 4)]),
        (m, planes - 3, 3, up.at[pl.ds(7, 3)]),
        (b, planes - 4, 4, up.at[pl.ds(10, 4)]),
        (vi, planes - 1, 1, up.at[pl.ds(14, 1)]),
    )
    copies = [
        pltpu.make_async_copy(ref.at[pl.ds(start, count)], target, sems.at[index])
        for index, (ref, start, count, target) in enumerate(jobs)
    ]
    run_copies(col_copies + copies)
    upper = iota((8, depth), 0) >= 4
    first = iota((8, depth), 0) == 0
    down[14:16] = jnp.zeros((2, columns, depth), F32)
    for copy in col_copies:
        copy.wait()

    def plane(index, _):
        before = jnp.maximum(index - 1, 0)
        keep = jnp.where(index > 0, 1.0, 0.0)
        for side in range(2):
            svi, svx, svd, sp, sm, sb = (strips.at[side, field] for field in range(6))
            div = (
                (svi[index] - keep * svi[before])
                + (svx[index] - row_before(svx[index]))
                + (svd[index] - lane_before(svd[index]))
            )
            turned_div = half_turn(div)
            turned_b = half_turn(sb[index])
            if side == 0:
                low[index, 0:8, :] = jnp.where(upper, turned_div, sp[index])
                low[index, 8:16, :] = jnp.where(upper, turned_b, sm[index])
            else:
                edge = jnp.where(first, pltpu.roll(svx[index], 1, 0), turned_div)
                high[index, 0:8, :] = jnp.where(upper, sp[index], edge)
                high[index, 8:16, :] = jnp.where(upper, sm[index], turned_b)
        return 0

    lax.fori_loop(0, planes, plane, 0, unroll=8)
    outs = run_copies(
        [
            pltpu.make_async_copy(low, low_out, out_sems.at[0]),
            pltpu.make_async_copy(high, high_out, out_sems.at[1]),
        ]
    )
    for copy in copies[:6]:
        copy.wait()
    last = columns - 1
    for base, out, line in ((0, down, 13), (3, up, 15)):
        for step in range(1, 4):
            div_i = vel[base, step]
            if base or step > 1:
                div_i = div_i - vel[base, step - 1]
            vx_now = vel[base + 1, step]
            vd_now = vel[base + 2, step]
            out[3 + step] = div_i + (vx_now - row_before(vx_now)) + (vd_now - lane_before(vd_now))
            out[line, step - 1 : step, :] = vel[base + 1, step, last : last + 1, :]
    for copy in copies[6:]:
        copy.wait()
    even = lax.axis_index("inline") % 2 == 0
    outs.append(Either(even, up, down, (), near_out, out_sems.at[2]))
    outs.append(Either(even, down, up, (), far_out, out_sems.at[3]))
    run_copies(outs[2:])
    for copy in outs:
        copy.wait()


def edge_pack(p, vi, vx, vd, m, b):
    planes, columns, depth = p.shape
    cols = (planes, 16, depth)
    sheets = (16, columns, depth)
    return pl.pallas_call(
        edge_pack_kernel,
        out_shape=tuple(jax.ShapeDtypeStruct(shape, F32) for shape in (cols, cols, sheets, sheets)),
        in_specs=[ANY] * 6,
        out_specs=(ANY,) * 4,
        scratch_shapes=[
            pltpu.VMEM((2, 6, planes, 8, depth), F32),
            pltpu.VMEM(cols, F32),
            pltpu.VMEM(cols, F32),
            pltpu.VMEM(sheets, F32),
            pltpu.VMEM(sheets, F32),
            pltpu.VMEM((6, 4, columns, depth), F32),
            pltpu.SemaphoreType.DMA((2, 6)),
            pltpu.SemaphoreType.DMA((13,)),
            pltpu.SemaphoreType.DMA((4,)),
        ],
        compiler_params=pltpu.CompilerParams(vmem_limit_bytes=VMEM_LIMIT),
    )(p, vi, vx, vd, m, b)


def corner_rows(side):
    entries = []
    for z in range(2):
        for di in range(1, HALO):
            entries += [(kind, z, di, dj) for dj in range(1, HALO + 1 - di) for kind in "pb"]
            entries += [(kind, z, di, dj) for dj in range(1, HALO - di) for kind in "dm"]
            if side == 1:
                entries.append(("line", z, di, 0))
    return entries + [("first", 0, 0, dj) for dj in range(1, HALO)]


CORNER_ROWS = 48


def corner_pack_kernel(near, far, low_cols, high_cols, vi, low_out, high_out, dn, upv, row0, vi_last, sems):
    columns, depth = near.shape[1:]
    planes = vi.shape[0]
    copies = []
    even = lax.axis_index("inline") % 2 == 0
    for side, start in ((0, 0), (1, columns - 8)):
        window = pl.ds(start, 8)
        copies += [
            Either(even, near, far, (pl.ds(0, 13), window), dn.at[side], sems.at[side, 0]),
            Either(even, far, near, (pl.ds(0, 15), window), upv.at[side], sems.at[side, 1]),
            pltpu.make_async_copy(vi.at[planes - 1, window, :], vi_last.at[side], sems.at[side, 2]),
            pltpu.make_async_copy(
                (low_cols, high_cols)[side].at[0, pl.ds(0, 8), :], row0.at[side], sems.at[side, 3]
            ),
        ]
    lines = [
        Either(even, far, near, (15, pl.ds(0, 8)), dn.at[2, 0], sems.at[2, 0]),
        Either(even, near, far, (13, pl.ds(0, 8)), dn.at[2, 1], sems.at[2, 1]),
    ]
    run_copies(copies + lines)
    for copy in copies + lines:
        copy.wait()
    has_before = lax.axis_index("inline") > 0
    for side, out in ((0, low_out), (1, high_out)):
        out[40:48, :] = jnp.zeros((8, depth), F32)
        for row, (kind, z, di, dj) in enumerate(corner_rows(side)):
            col = dj - 1 if side == 0 else 8 - dj
            at = slice(col, col + 1)
            if kind == "first":
                place = 3 + dj if side == 0 else 4 - dj
                value = row0[side, place : place + 1, :]
                value = value - jnp.where(has_before, upv[side, 14, at, :], 0.0)
            elif kind == "line":
                line = di - 1 if z else 3 - di
                value = dn[2, z, line : line + 1, :]
            elif z:
                value = dn[side, {"p": 0, "d": 4, "m": 7, "b": 10}[kind] + di - 1, at, :]
                if kind == "d" and di == 1:
                    value = value - vi_last[side, at, :]
            else:
                value = upv[side, {"p": 4, "d": 7, "m": 10, "b": 14}[kind] - di, at, :]
            out[row : row + 1, :] = value


def corner_pack(near, far, low_cols, high_cols, vi):
    depth = near.shape[2]
    out = jax.ShapeDtypeStruct((CORNER_ROWS, depth), F32)
    return pl.pallas_call(
        corner_pack_kernel,
        out_shape=(out, out),
        in_specs=[ANY] * 5,
        out_specs=(VMEM, VMEM),
        scratch_shapes=[
            pltpu.VMEM((3, 13, 8, depth), F32),
            pltpu.VMEM((2, 15, 8, depth), F32),
            pltpu.VMEM((2, 8, depth), F32),
            pltpu.VMEM((2, 8, depth), F32),
            pltpu.SemaphoreType.DMA((3, 4)),
        ],
        compiler_params=pltpu.CompilerParams(vmem_limit_bytes=VMEM_LIMIT),
    )(near, far, low_cols, high_cols, vi)


def split3(value):
    high = value.astype(BF16)
    rest = value - high.astype(F32)
    mid = rest.astype(BF16)
    low = (rest - mid.astype(F32)).astype(BF16)
    return high, mid, low


def route_kernel(rounds, n_inline, n_xline, block, traces, resample, owner, cell, out, places):
    planes, columns, depth = block
    nodes = traces.shape[0]
    devices = n_inline * n_xline
    sources = lax.dot_general(
        resample[...],
        traces[...],
        (((1,), (1,)), ((), ())),
        precision=lax.Precision.HIGHEST,
        preferred_element_type=F32,
    )
    own, at = owner[...], cell[...].reshape(1, nodes)
    own_x, own_i = own // n_inline, own % n_inline
    at_i, at_j = at // (columns * depth), (at // depth) % columns
    target = iota((devices, 1), 0)
    rel_i = (own_i - target % n_inline) * planes + at_i
    rel_j = (own_x - target // n_inline) * columns + at_j
    off_i = jnp.maximum(jnp.maximum(-rel_i, rel_i - (planes - 1)), 0)
    off_j = jnp.maximum(jnp.maximum(-rel_j, rel_j - (columns - 1)), 0)
    member = off_i + off_j <= REACH
    member_f = jnp.where(member, 1.0, 0.0)
    earlier = jnp.where(iota((nodes, nodes), 0) < iota((nodes, nodes), 1), 1.0, 0.0).astype(BF16)
    place = jnp.dot(member_f.astype(BF16), earlier, preferred_element_type=F32)
    places[...] = jnp.where(member, place, -1.0)
    most = jnp.max(jnp.sum(member_f, axis=1, keepdims=True))
    flag = jnp.where(most > SLOTS, FLAG, 0.0)

    high, mid, low = split3(sources)
    digits = jnp.concatenate([at % 256, (at // 256) % 256, at // 65536, own + 1], 0).astype(F32).astype(BF16)
    none = jnp.zeros(digits.shape, F32).astype(BF16)
    data = jnp.concatenate([high, digits, mid, none, low, none], 0)
    slot = iota((SLOTS, nodes), 0).astype(F32)
    raised = jnp.where(iota((8, SLOTS), 0) == 4, flag, 0.0)

    def one(index, _):
        device = index % devices
        first = (index // devices + rounds[0]) * SLOTS
        row = places[pl.ds(device, 1), :] - first.astype(F32)
        chosen = jnp.where(slot == row, 1.0, 0.0).astype(BF16)
        packed = lax.dot_general(
            data, chosen, (((1,), (1,)), ((), ())), preferred_element_type=F32
        )
        out[pl.ds(pl.multiple_of(index * 8, 8), 8), :] = (
            packed[0:8] + packed[8:16] + packed[16:24] + raised
        )
        return 0

    lax.fori_loop(0, len(rounds) * devices, one, 0, unroll=16)


def route(traces, resample, owner, cell, rounds, block):
    n_inline, n_xline = lax.axis_size("inline"), lax.axis_size("xline")
    devices = n_inline * n_xline
    nodes = traces.shape[0]
    return pl.pallas_call(
        functools.partial(route_kernel, rounds, n_inline, n_xline, block),
        out_shape=jax.ShapeDtypeStruct((len(rounds) * devices * 8, SLOTS), F32),
        in_specs=[VMEM] * 4,
        out_specs=VMEM,
        scratch_shapes=[pltpu.VMEM((devices, nodes), F32)],
        compiler_params=pltpu.CompilerParams(vmem_limit_bytes=VMEM_LIMIT),
    )(traces, resample, owner, cell)


def step_kernel(
    rounds, n_inline, n_xline, *refs
):
    if rounds:
        more, *refs = refs
    (recv, p, vi, vx, vd, m, b, near, far, right, left, corner_r, corner_l,
    p_out, vi_out, vx_out, vd_out,
    pb, div, mb, bb, inj, v0, v1, v2, p4, bs, lines, strip_r, strip_l, cor_r, cor_l,
    lists, codes_v, later_v, parity, counts_v, codes, late_codes, counts, batches, bk, sems, list_sems, out_sems) = refs
    planes, columns, depth = p.shape
    rows = columns + 8
    devices = n_inline * n_xline
    at_i, at_x = lax.axis_index("inline"), lax.axis_index("xline")
    own_p, own_c = pl.ds(4, planes), pl.ds(0, columns)
    lane_tiles = depth // 128
    inj_planes = planes + 2 * REACH
    dummy = lane_tiles * inj_planes * rows // 2

    nothing = devices * PARTS
    arrived = lists.at[pl.ds(0, devices * 8), :]
    lists[pl.ds(devices * 8, 8), :] = jnp.zeros((8, SLOTS), F32)
    first_list = pltpu.make_async_copy(recv, arrived, list_sems.at[0])
    first_list.start()
    jobs = (
        (vi, v0.at[pl.ds(1, planes)]),
        (vx, v1),
        (vd, v2),
        (b, bb.at[own_p, own_c, :]),
        (right, strip_r),
        (left, strip_l),
        (p, pb.at[0, own_p, own_c, :]),
        (m, mb.at[own_p, own_c, :]),
        (corner_r, cor_r),
        (corner_l, cor_l),
    )
    up_jobs = (
        (pl.ds(0, 4), pb.at[0, pl.ds(0, 4), own_c, :]),
        (pl.ds(4, 3), div.at[pl.ds(1, 3), own_c, :]),
        (pl.ds(7, 3), mb.at[pl.ds(1, 3), own_c, :]),
        (pl.ds(10, 4), bb.at[pl.ds(0, 4), own_c, :]),
        (14, v0.at[0]),
        ((15, pl.ds(0, 8)), lines.at[0]),
    )
    down_jobs = (
        (pl.ds(0, 4), pb.at[0, pl.ds(planes + 4, 4), own_c, :]),
        (pl.ds(4, 3), div.at[pl.ds(planes + 4, 3), own_c, :]),
        (pl.ds(7, 3), mb.at[pl.ds(planes + 4, 3), own_c, :]),
        (pl.ds(10, 3), bb.at[pl.ds(planes + 4, 3), own_c, :]),
        ((13, pl.ds(0, 8)), lines.at[1]),
    )
    even = at_i % 2 == 0
    copies = [pltpu.make_async_copy(src, dst, sems.at[index]) for index, (src, dst) in enumerate(jobs)]
    ups = [
        Either(even, far, near, index, dst, sems.at[10 + job]) for job, (index, dst) in enumerate(up_jobs)
    ]
    downs = [
        Either(even, near, far, index, dst, sems.at[16 + job]) for job, (index, dst) in enumerate(down_jobs)
    ]
    early = run_copies(copies[:6] + [ups[4]])
    late = copies[6:] + ups[:4] + ups[5:] + downs

    def clear(index, _):
        inj[pl.ds(pl.multiple_of(index * rows * STEPS, 8), rows * STEPS), :] = jnp.zeros(
            (rows * STEPS, 128), F32
        )
        return 0

    lax.fori_loop(0, lane_tiles * inj_planes, clear, 0)
    first_list.wait()
    sub = iota((8, SLOTS), 0)
    lane = iota((8, SLOTS), 1)

    low_i, high_i = at_i == 0, at_i == n_inline - 1
    low_x, high_x = at_x == 0, at_x == n_xline - 1
    keep_x = jnp.where(low_x, 0.0, 1.0)
    end_x = jnp.where(high_x, 0.0, 1.0)
    top = iota((8, depth), 0) == 0
    top_own = iota((columns, depth), 0) == 0
    edge = slice(columns, columns + 8)
    upper = iota((8, depth), 0) >= 4
    square = COURANT * COURANT

    def own_plane(index):
        plane = index + 4
        a_l, b_l = strip_l[index, 0:8, :], strip_l[index, 8:16, :]
        a_r, b_r = strip_r[index, 0:8, :], strip_r[index, 8:16, :]
        now_x, now_d = v1[index], v2[index]
        pb[0, plane, edge, :] = jnp.where(upper, a_l, end_x * a_r)
        mb[plane, edge, :] = jnp.where(upper, b_l, end_x * b_r)
        turned = half_turn(jnp.where(upper, a_r, a_l))
        div[plane, edge, :] = COURANT * (turned - jnp.where(top, now_x[columns - 1 : columns, :], 0.0))
        buoy = square * half_turn(jnp.where(upper, b_r, keep_x * b_l))
        bs[plane, edge, :] = buoy
        bk[plane, edge, :] = lane_before(buoy)
        x_before = jnp.where(top_own, keep_x * a_l[0:1, :], pltpu.roll(now_x, 1, 0))
        div[plane, own_c, :] = COURANT * (
            (v0[index + 1] - v0[index]) + (now_x - x_before) + (now_d - lane_before(now_d))
        )
        buoy = square * bb[plane, own_c, :]
        bs[plane, own_c, :] = buoy
        bk[plane, own_c, :] = lane_before(buoy)

    def start_block():
        for copy in early:
            copy.wait()
        run_copies(late)

        @pl.when(low_i)
        def _():
            v0[0] = jnp.zeros((columns, depth), F32)

    def one_round(turn, _):
        if rounds:
            @pl.when(turn > 0)
            def _():
                copy = pltpu.make_async_copy(more.at[jnp.maximum(turn - 1, 0)], arrived, list_sems.at[0])
                copy.start()
                copy.wait()

        digit0 = lists[pl.ds(4, devices, stride=8), :]
        digit0 = digit0 - jnp.where(digit0 >= FLAG, FLAG, 0.0)
        digit1 = lists[pl.ds(5, devices, stride=8), :]
        digit2 = lists[pl.ds(6, devices, stride=8), :]
        named = lists[pl.ds(7, devices, stride=8), :]
        cell = (digit0 + 256.0 * digit1 + 65536.0 * digit2).astype(jnp.int32)
        own = jnp.maximum(named.astype(jnp.int32) - 1, 0)
        rel_i = (own % n_inline - at_i) * planes + cell // (columns * depth)
        rel_j = (own // n_inline - at_x) * columns + (cell // depth) % columns
        k = cell % depth
        flat = (rel_i + REACH) * rows + jnp.where(rel_j < 0, rel_j + rows, rel_j)
        tile = (k // 128) * (inj_planes * rows // 2) + flat // 2
        slot = iota(tile.shape, 1)
        code = tile * SLOTS + ((k - slot) & (SLOTS - 1))
        parity[...] = flat % 2
        valid = named > 0.0
        tile = jnp.where(valid, tile, -1)
        clash = jnp.zeros(tile.shape, jnp.int32)
        for back in range(1, BATCH):
            same = (pltpu.roll(tile, back, 1) == tile) & (slot % BATCH >= back)
            clash = jnp.where(same, 1, clash)
        now = valid & (clash == 0)
        later = valid & (clash == 1)
        codes_v[0:devices, :] = jnp.where(now, code, dummy * SLOTS)
        codes_v[devices:, :] = jnp.full((8, SLOTS), dummy * SLOTS, jnp.int32)
        later_v[...] = jnp.where(later, code, dummy * SLOTS)
        count = jnp.sum(jnp.where(valid, 1.0, 0.0), axis=1, keepdims=True).astype(jnp.int32)
        put_off = jnp.where(later, 1, 0)
        for ahead in (4, 2, 1):
            put_off = jnp.maximum(put_off, pltpu.roll(put_off, SLOTS - ahead, 1))
        any_off = jnp.max(put_off.astype(F32), axis=1, keepdims=True).astype(jnp.int32)
        counts_v[...] = jnp.where(
            slot % BATCH == 0, put_off, jnp.where(slot == 1, count, any_off)
        )
        to_smem = run_copies(
            [
                pltpu.make_async_copy(codes_v, codes, list_sems.at[1]),
                pltpu.make_async_copy(counts_v, counts, list_sems.at[2]),
                pltpu.make_async_copy(later_v, late_codes, list_sems.at[3]),
            ]
        )
        for copy in to_smem:
            copy.wait()

        def one_list(source, total):
            rows8 = pl.ds(pl.multiple_of(source * 8, 8), 8)
            tile8 = lists[rows8, :]
            odd = jnp.broadcast_to(parity[pl.ds(source, 1), :], (8, SLOTS))
            mine = jnp.where(sub < 4, tile8, half_turn(tile8))
            lists[rows8, :] = jnp.where(sub // 4 == odd, COURANT * mine, 0.0)
            for part in range(PARTS):
                batches[total + part] = source * PARTS + part
            return total + (counts[source, 1] + BATCH - 1) // BATCH

        total = lax.fori_loop(0, devices, one_list, 0, unroll=4)

        def pad(index, _):
            for extra in range(GROUPS):
                batches[total + index * GROUPS + extra] = nothing
            return 0

        lax.fori_loop(0, jnp.maximum(planes - total // GROUPS, 1), pad, 0)

        def spread(values, code, slot_at):
            alone = jnp.where(lane == slot_at, values, 0.0)
            return pltpu.roll(alone, code & (SLOTS - 1), 1)

        def prepare(index):
            name = batches[index]
            source, base = name >> PART_BITS, (name & (PARTS - 1)) * BATCH
            values = lists[pl.ds(pl.multiple_of(source * 8, 8), 8), :]
            found = [codes[source, base + unit] for unit in range(BATCH)]
            rows_at = [pl.ds(pl.multiple_of((code >> 7) * 8, 8), 8) for code in found]
            return [spread(values, code, base + unit) for unit, code in enumerate(found)], rows_at

        def batch(index, _):
            ready = [prepare(index * GROUPS + group) for group in range(GROUPS)]
            for adds, rows_at in ready:
                sums = [inj[row, :] + add for row, add in zip(rows_at, adds)]
                for row, value in zip(rows_at, sums):
                    inj[row, :] = value
            own_plane(jnp.minimum(index, planes - 1))
            return 0

        if not rounds:
            start_block()
        turns = jnp.maximum((total + GROUPS - 1) // GROUPS, planes)
        lax.fori_loop(0, turns, batch, 0)

        def put_off_list(source, _):
            @pl.when(counts[source, 2] > 0)
            def _():
                values = lists[pl.ds(pl.multiple_of(source * 8, 8), 8), :]

                def part_of(part, _):
                    @pl.when(counts[source, part * BATCH] > 0)
                    def _():
                        for unit in range(BATCH):
                            slot_at = part * BATCH + unit
                            code = late_codes[source, slot_at]
                            row = pl.ds(pl.multiple_of((code >> 7) * 8, 8), 8)
                            inj[row, :] += spread(values, code, slot_at)

                    return 0

                lax.fori_loop(0, PARTS, part_of, 0)

            return 0

        lax.fori_loop(0, devices, put_off_list, 0)
        return 0

    if rounds:
        start_block()
        lax.fori_loop(0, 1 + rounds, one_round, 0)
    else:
        one_round(0, 0)
    for copy in late:
        copy.wait()

    own_line = v1[0, columns - 1 : columns, :]
    for side, box in ((0, cor_r), (1, cor_l)):
        for row, (kind, z, di, dj) in enumerate(corner_rows(side)):
            plane = planes + 3 + di if z else 4 - di
            spot = columns + dj - 1 if side == 0 else rows - dj
            at = slice(spot, spot + 1)
            value = box[row : row + 1, :]
            line = di - 1 if z else 3 - di
            if kind == "p":
                pb[0, plane, at, :] = value
            elif kind == "b":
                bb[plane, at, :] = value
            elif kind == "m":
                mb[plane, at, :] = value
            elif kind == "line":
                fix = jnp.where(top_own, keep_x * value, 0.0)
                if z and di == 1:
                    fix = fix + v0[planes]
                div[plane, own_c, :] = COURANT * (div[plane, own_c, :] - fix)
            else:
                if side == 0 and dj == 1:
                    value = value - (own_line if kind == "first" else lines[z, line : line + 1, :])
                div[plane, at, :] = COURANT * value

    for first in (0, planes + 4):
        @pl.when(low_x)
        def _(first=first):
            bb[first : first + 4, columns + 4 :, :] = jnp.zeros((4, 4, depth), F32)

        @pl.when(high_x)
        def _(first=first):
            pb[0, first : first + 4, columns : columns + 4, :] = jnp.zeros((4, 4, depth), F32)
            mb[first : first + 4, columns : columns + 4, :] = jnp.zeros((4, 4, depth), F32)

    @pl.when(low_i)
    def _():
        bb[0:4] = jnp.zeros((4, rows, depth), F32)

    @pl.when(high_i)
    def _():
        pb[0, planes + 4 :] = jnp.zeros((4, rows, depth), F32)
        mb[planes + 4 :] = jnp.zeros((4, rows, depth), F32)

    for plane in (0, 1, 2, 3, planes + 4, planes + 5, planes + 6):
        buoy = square * bb[plane]
        bs[plane] = buoy
        bk[plane] = lane_before(buoy)

    def advance(step, plane, flux_before):
        now, after, buoy = pb[step, plane], pb[step, plane + 1], bs[plane]
        flux_i = buoy * (after - now)
        flux_x = buoy * (pltpu.roll(now, rows - 1, 0) - now)
        change_d = buoy * (lane_after(now) - now) - bk[plane] * (now - pltpu.roll(now, 1, 1))
        change = (
            (flux_i - flux_before)
            + (flux_x - pltpu.roll(flux_x, 1, 0))
            + change_d
        )
        new_div = div[plane] - change
        source = jnp.concatenate(
            [
                inj[pl.ds((part * inj_planes + plane - 1) * rows * STEPS + step, rows, stride=STEPS), :]
                for part in range(lane_tiles)
            ],
            1,
        )
        return flux_i, new_div, now - mb[plane] * (new_div - source)

    for step in range(STEPS - 1):
        def one_plane(plane, flux_before, step=step):
            flux_i, new_div, new_p = advance(step, plane, flux_before)
            div[plane] = new_div
            pb[step + 1, plane] = new_p
            return flux_i

        start = 1 + step
        flux = bs[step] * (pb[step, start] - pb[step, step])
        lax.fori_loop(start, planes + 7 - step, one_plane, flux, unroll=UNROLL)

    last = STEPS - 1

    def total(plane):
        return (pb[0, plane] + pb[1, plane]) + (pb[2, plane] + pb[3, plane])

    def last_plane(index, flux_before):
        plane = index + 4
        flux_i, _, new_p = advance(last, plane, flux_before)
        p4[index] = new_p[:columns]
        here, there = total(plane), total(plane + 1)
        scaled = (1.0 / COURANT) * bs[plane, own_c, :]
        mine = here[:columns]
        v0[index + 1] = v0[index + 1] - scaled * (there[:columns] - mine)
        v1[index] = v1[index] - scaled * (pltpu.roll(here, rows - 1, 0)[:columns] - mine)
        v2[index] = v2[index] - scaled * (lane_after(mine) - mine)
        return flux_i

    flux = bs[3] * (pb[last, 4] - pb[last, 3])
    chunk = planes // 8
    outs = []
    for part in range(8):
        flux = lax.fori_loop(part * chunk, (part + 1) * chunk, last_plane, flux, unroll=UNROLL)
        window = pl.ds(part * chunk, chunk)
        outs += run_copies(
            [
                pltpu.make_async_copy(src, dst.at[window], out_sems.at[part, index])
                for index, (src, dst) in enumerate(
                    (
                        (p4.at[window], p_out),
                        (v0.at[pl.ds(part * chunk + 1, chunk)], vi_out),
                        (v1.at[window], vx_out),
                        (v2.at[window], vd_out),
                    )
                )
            ]
        )
    for copy in outs:
        copy.wait()


def step_all(recv, more, fields, halos):
    p = fields[0]
    planes, columns, depth = p.shape
    n_inline, n_xline = lax.axis_size("inline"), lax.axis_size("xline")
    devices = n_inline * n_xline
    rows = columns + 8
    full = (planes + 8, rows, depth)
    block = (planes, columns, depth)
    inj_rows = (depth // 128) * (planes + 2 * REACH) * rows * STEPS
    return pl.pallas_call(
        functools.partial(step_kernel, 0 if more is None else more.shape[0], n_inline, n_xline),
        out_shape=tuple(jax.ShapeDtypeStruct(block, F32) for _ in range(4)),
        in_specs=[ANY] * (13 if more is None else 14),
        out_specs=(ANY,) * 4,
        scratch_shapes=[
            pltpu.VMEM((STEPS,) + full, F32),
            pltpu.VMEM(full, F32),
            pltpu.VMEM(full, F32),
            pltpu.VMEM(full, F32),
            pltpu.VMEM((inj_rows + 8, 128), F32),
            pltpu.VMEM((planes + 1, columns, depth), F32),
            pltpu.VMEM(block, F32),
            pltpu.VMEM(block, F32),
            pltpu.VMEM(block, F32),
            pltpu.VMEM(full, F32),
            pltpu.VMEM((2, 8, depth), F32),
            pltpu.VMEM((planes, 16, depth), F32),
            pltpu.VMEM((planes, 16, depth), F32),
            pltpu.VMEM((CORNER_ROWS, depth), F32),
            pltpu.VMEM((CORNER_ROWS, depth), F32),
            pltpu.VMEM((devices * 8 + 8, SLOTS), F32),
            pltpu.VMEM((devices + 8, SLOTS), jnp.int32),
            pltpu.VMEM((devices, SLOTS), jnp.int32),
            pltpu.VMEM((devices, SLOTS), jnp.int32),
            pltpu.VMEM((devices, SLOTS), jnp.int32),
            pltpu.SMEM((devices + 8, SLOTS), jnp.int32),
            pltpu.SMEM((devices, SLOTS), jnp.int32),
            pltpu.SMEM((devices, SLOTS), jnp.int32),
            pltpu.SMEM((devices * PARTS + (planes + 2) * GROUPS,), jnp.int32),
            pltpu.VMEM(full, F32),
            pltpu.SemaphoreType.DMA((21,)),
            pltpu.SemaphoreType.DMA((4,)),
            pltpu.SemaphoreType.DMA((8, 4)),
        ],
        compiler_params=pltpu.CompilerParams(vmem_limit_bytes=VMEM_LIMIT),
    )(*(() if more is None else (more,)), recv, *fields, *halos)


def shards(pressure, vel_inline, vel_xline, vel_depth, modulus, buoyancy, traces, owner, node_cell, resample):
    fields = (pressure, vel_inline, vel_xline, vel_depth, modulus, buoyancy)
    block = pressure.shape
    devices = lax.axis_size("xline") * lax.axis_size("inline")
    nodes = traces.shape[0]
    capacity = max(4, 5 * nodes // (2 * devices))
    most = min(nodes, 9 * capacity)
    rounds = -(-most // SLOTS)

    low_cols, high_cols, near_send, far_send = edge_pack(*fields)
    right = rotate(low_cols, "xline", -1)
    left = rotate(high_cols, "xline", 1)
    count = lax.axis_size("inline")
    near = lax.ppermute(near_send, "inline", [(source, source ^ 1) for source in range(count)])
    far = lax.ppermute(
        far_send,
        "inline",
        [(source, source if source in (0, count - 1) else ((source - 1) ^ 1) + 1) for source in range(count)],
    )

    owner_row, cell_row = owner.reshape(1, nodes), node_cell
    send = route(traces, resample, owner_row, cell_row, (0,), block)

    def exchange(packed):
        return lax.all_to_all(packed, ("xline", "inline"), split_axis=0, concat_axis=0, tiled=True)

    low_corner, high_corner = corner_pack(near, far, low_cols, high_cols, vel_inline)
    corner_r = rotate(low_corner, "xline", -1)
    corner_l = rotate(high_corner, "xline", 1)
    recv = exchange(send.reshape(devices, 8, SLOTS)).reshape(devices * 8, SLOTS)
    over = jnp.max(recv) >= FLAG / 2
    halos = (near, far, right, left, corner_r, corner_l)

    def spill():
        packed = route(traces, resample, owner_row, cell_row, tuple(range(1, rounds)), block)
        packed = packed.reshape(rounds - 1, devices, 8, SLOTS)
        more = jnp.stack([exchange(packed[turn]) for turn in range(rounds - 1)])
        return step_all(recv, more.reshape(rounds - 1, devices * 8, SLOTS), fields, halos)

    def plain():
        return step_all(recv, None, fields, halos)

    return lax.cond(over, spill, plain) if rounds > 1 else plain()


def solution(mesh):
    field = P("inline", "xline", None)
    nodes = ("xline", "inline")
    return jax.shard_map(
        shards,
        mesh=mesh,
        in_specs=(field,) * 6 + (P(nodes, None), P(nodes, None), P(nodes), P()),
        out_specs=(field,) * 4,
        check_vma=False,
    )
```

profile of v0, /device:TPU:0, one launch (start us, length us, event | category | flops | bytes accessed | tf_op | source)
XLA Modules:
  0.0 74.1 jit_solution(4598436652235276334)
XLA Ops:
  0.6 5.1 %shard_map.138 = (f32[32,16,256]{2,1,0:T(8,128)}, f32[32,16,256]{2,1,0:T(8,128)}, f32[16,64,256]{2,1,0:T(8,128)}, f32[16,64,256]{2,1,0:T(8,128)}) custom-call(f32[32,64,256]{2,1,0:T(8,128)} %p.1, f32[32,64,256]{2,1,0:T(8,128)} %vi.3, f32[32,64,256]{2,1,0:T(8,128)} %vx.1, f32[32,64,256]{2,1,0:T(8,128)} %vd.1, f32[32,64,256]{2,1,0:T(8,128)} %m.1, f32[32,64,256]{2,1,0:T(8,128)} %b.1), custom_call_target="tpu_custom_call" | custom-call | tf_op jit(solution)/shard_map/pallas_call | solution.py:170
  5.7 0.5 collective-permute-start
  6.2 9.4 %collective-permute-start.1 = (f32[16,64,256]{2,1,0:T(8,128)}, f32[16,64,256]{2,1,0:T(8,128)}, u32[]{:S(2)}, u32[]{:S(2)}) collective-permute-start(f32[16,64,256]{2,1,0:T(8,128)} %get-tuple-element.101), channel_id=1, source_target_pairs={{0,0},{1,2},{2,1},{3,4},{4,3},{5,6},{6,5},{7,7},{8,8},{9,10},{10,9... | collective-permute-start | bytes 3145736 | tf_op jit(solution)/shard_map/ppermute | solution.py:759
  15.7 3.5 %collective-permute-start.2 = (f32[32,16,256]{2,1,0:T(8,128)}, f32[32,16,256]{2,1,0:T(8,128)}, u32[]{:S(2)}, u32[]{:S(2)}) collective-permute-start(f32[32,16,256]{2,1,0:T(8,128)} %get-tuple-element.102.low_cols), channel_id=1, source_target_pairs={{0,24},{8,0},{16,8},{24,16},{1,25},{9,1},{17,9},{25,17},{2,26},{10... | collective-permute-start | bytes 1572872 | tf_op jit(solution)/shard_map/ppermute | solution.py:31
  19.2 0.0 collective-permute-start.3
  19.2 5.6 %shard_map.137 = f32[256,128]{1,0:T(8,128)} custom-call(f32[768,512]{1,0:T(8,128)} %traces.1, f32[4,512]{1,0:T(4,128)} %resample.1, s32[1,768]{1,0:T(1,128)} %bitcast.20, s32[768]{0:T(1024)} %cell.1), custom_call_target="tpu_custom_call" | custom-call | tf_op jit(solution)/shard_map/pallas_call | solution.py:329
  24.8 6.0 %all-to-all-start.4 = ((f32[32,8,128]{2,1,0:T(8,128)}), f32[32,8,128]{2,1,0:T(8,128)}, u32[]{:S(2)}, u32[]{:S(2)}) async-start(f32[32,8,128]{2,1,0:T(8,128)} %bitcast.15), calls=%async_computation.4 | async-start | bytes 262144 | tf_op jit(solution)/shard_map/all_to_all | solution.py:769
  30.8 0.0 collective-permute-done.near
  30.8 0.0 collective-permute-done.1.far
  30.8 1.9 %shard_map.139 = (f32[48,256]{1,0:T(8,128)}, f32[48,256]{1,0:T(8,128)}) custom-call(f32[16,64,256]{2,1,0:T(8,128)} %collective-permute-done.near, f32[16,64,256]{2,1,0:T(8,128)} %collective-permute-done.1.far, f32[32,16,256]{2,1,0:T(8,128)} %get-tuple-element.102.low_cols, f32[32,16,256]{2,1,0:T(8,128)} %get-tuple-element.103.high_cols, f32[32,64,256]{2,1,0:T(8,128)} %vi.3), custom_call_target="tpu_custom_call" | custom-call | tf_op jit(solution)/shard_map/pallas_call | solution.py:251
  32.7 2.6 %collective-permute-start.4 = (f32[48,256]{1,0:T(8,128)}, f32[48,256]{1,0:T(8,128)}, u32[]{:S(2)}, u32[]{:S(2)}) collective-permute-start(f32[48,256]{1,0:T(8,128)} %get-tuple-element.104), channel_id=1, source_target_pairs={{0,24},{8,0},{16,8},{24,16},{1,25},{9,1},{17,9},{25,17},{2,26},{10... | collective-permute-start | bytes 147464 | tf_op jit(solution)/shard_map/ppermute | solution.py:31
  35.4 0.0 collective-permute-start.5
  35.4 3.7 %all-to-all-done.4 = f32[32,8,128]{2,1,0:T(8,128)} async-done(((f32[32,8,128]{2,1,0:T(8,128)}), f32[32,8,128]{2,1,0:T(8,128)}, u32[]{:S(2)}, u32[]{:S(2)}) %all-to-all-start.4) | async-done | bytes 131104 | tf_op jit(solution)/shard_map/all_to_all | solution.py:769
  39.1 1.6 %reduce_max.9 = f32[]{:T(128)} reduce(f32[32,8,128]{2,1,0:T(8,128)} %all-to-all-done.4, f32[]{:T(128)} %constant.0.clone.1), dimensions={0,1,2}, to_apply=%region_0.0 | reduce | flops 32767 | bytes 131080 | tf_op jit(solution)/shard_map/reduce_max | solution.py:775
  41.3 0.0 collective-permute-done.2
  41.3 0.0 collective-permute-done.3
  41.4 0.0 collective-permute-done.4
  41.4 0.0 collective-permute-done.5
  41.4 32.5 %conditional.1 = ((f32[32,64,256]{2,1,0:T(8,128)}, f32[32,64,256]{2,1,0:T(8,128)}, f32[32,64,256]{2,1,0:T(8,128)}, f32[32,64,256]{2,1,0:T(8,128)})) conditional(s32[]{:T(128)} %convert_element_type.3, (f32[256,128]{1,0:T(8,128)}, f32[32,64,256]{2,1,0:T(8,128)}, f32[32,64,256]{2,1,0:T(8,128)}, f32[32,64,256]{2,1,0:T(8,128)}, f32[32,64,256]{2,1,0:T(8,128)}, ...), branch_computations={%region_1.0_spmd, %region_2.0_spmd} | conditional | flops 393216 | bytes 3145736 | solution.py:787
  41.4 32.3 %branch_0_fun.1 = (f32[32,64,256]{2,1,0:T(8,128)}, f32[32,64,256]{2,1,0:T(8,128)}, f32[32,64,256]{2,1,0:T(8,128)}, f32[32,64,256]{2,1,0:T(8,128)}) custom-call(f32[256,128]{1,0:T(8,128)} %get-tuple-element.60.refs_0_, f32[32,64,256]{2,1,0:T(8,128)} %get-tuple-element.61.refs_1_, f32[32,64,256]{2,1,0:T(8,128)} %get-tuple-element.62.refs_2_, ...), custom_call_target="tpu_custom_call" | custom-call | tf_op jit(solution)/shard_map/cond/branch_0_fun/pallas_call | solution.py:706
Async XLA Ops:
  5.7 25.0 %collective-permute-start = (f32[16,64,256]{2,1,0:T(8,128)}, f32[16,64,256]{2,1,0:T(8,128)}, u32[]{:S(2)}, u32[]{:S(2)}) collective-permute-start(f32[16,64,256]{2,1,0:T(8,128)} %get-tuple-element.100), channel_id=1, source_target_pairs={{0,1},{1,0},{2,3},{3,2},{4,5},{5,4},{6,7},{7,6},{8,9},{9,8},{10,11... | collective-permute-start | bytes 3145736 | tf_op jit(solution)/shard_map/ppermute | solution.py:758
  6.2 24.5 %collective-permute-start.1 = (f32[16,64,256]{2,1,0:T(8,128)}, f32[16,64,256]{2,1,0:T(8,128)}, u32[]{:S(2)}, u32[]{:S(2)}) collective-permute-start(f32[16,64,256]{2,1,0:T(8,128)} %get-tuple-element.101), channel_id=1, source_target_pairs={{0,0},{1,2},{2,1},{3,4},{4,3},{5,6},{6,5},{7,7},{8,8},{9,10},{10,9... | collective-permute-start | bytes 3145736 | tf_op jit(solution)/shard_map/ppermute | solution.py:759
  15.7 25.7 %collective-permute-start.2 = (f32[32,16,256]{2,1,0:T(8,128)}, f32[32,16,256]{2,1,0:T(8,128)}, u32[]{:S(2)}, u32[]{:S(2)}) collective-permute-start(f32[32,16,256]{2,1,0:T(8,128)} %get-tuple-element.102.low_cols), channel_id=1, source_target_pairs={{0,24},{8,0},{16,8},{24,16},{1,25},{9,1},{17,9},{25,17},{2,26},{10... | collective-permute-start | bytes 1572872 | tf_op jit(solution)/shard_map/ppermute | solution.py:31
  19.2 22.2 %collective-permute-start.3 = (f32[32,16,256]{2,1,0:T(8,128)}, f32[32,16,256]{2,1,0:T(8,128)}, u32[]{:S(2)}, u32[]{:S(2)}) collective-permute-start(f32[32,16,256]{2,1,0:T(8,128)} %get-tuple-element.103.high_cols), channel_id=1, source_target_pairs={{0,8},{8,16},{16,24},{24,0},{1,9},{9,17},{17,25},{25,1},{2,10},{10... | collective-permute-start | bytes 1572872 | tf_op jit(solution)/shard_map/ppermute | solution.py:31
  24.8 14.3 %all-to-all-start.4 = ((f32[32,8,128]{2,1,0:T(8,128)}), f32[32,8,128]{2,1,0:T(8,128)}, u32[]{:S(2)}, u32[]{:S(2)}) async-start(f32[32,8,128]{2,1,0:T(8,128)} %bitcast.15), calls=%async_computation.4 | async-start | bytes 262144 | tf_op jit(solution)/shard_map/all_to_all | solution.py:769
  32.7 8.7 %collective-permute-start.4 = (f32[48,256]{1,0:T(8,128)}, f32[48,256]{1,0:T(8,128)}, u32[]{:S(2)}, u32[]{:S(2)}) collective-permute-start(f32[48,256]{1,0:T(8,128)} %get-tuple-element.104), channel_id=1, source_target_pairs={{0,24},{8,0},{16,8},{24,16},{1,25},{9,1},{17,9},{25,17},{2,26},{10... | collective-permute-start | bytes 147464 | tf_op jit(solution)/shard_map/ppermute | solution.py:31
  35.4 6.0 %collective-permute-start.5 = (f32[48,256]{1,0:T(8,128)}, f32[48,256]{1,0:T(8,128)}, u32[]{:S(2)}, u32[]{:S(2)}) collective-permute-start(f32[48,256]{1,0:T(8,128)} %get-tuple-element.105), channel_id=1, source_target_pairs={{0,8},{8,16},{16,24},{24,0},{1,9},{9,17},{17,25},{25,1},{2,10},{10... | collective-permute-start | bytes 147464 | tf_op jit(solution)/shard_map/ppermute | solution.py:31
where the time goes:
time: 75.5 us; the launch traced here: 74.1 us
  Pallas kernels  44.9 us (59%)
  starting transfers between devices  22.1 us (29%)
  waiting for transfers between devices  3.76 us (5%)
  other arithmetic  1.6 us (2%)
  between operations  1.52 us (2%)
    pallas_call x1, Pallas kernels, step_all(): pl.pallas_call(functools.partial(step_kernel, 0 if more is None else more...  32.3 us
    ppermute x1, starting transfers between devices, shards(): lax.ppermute(far_send, 'inline', [(source, source if source in (0, count...  9.44 us
    ppermute x4, starting transfers between devices, rotate(): lax.ppermute(value, axis, [(source, (source + steps) % count) for source...  6.12 us
    all_to_all x1, starting transfers between devices, exchange(): lax.all_to_all(packed, ('xline', 'inline'), split_axis=0, concat_axis=0,...  5.98 us
    pallas_call x1, Pallas kernels, route(): pl.pallas_call(functools.partial(route_kernel, rounds, n_inline, n_xline,...  5.62 us
    pallas_call x1, Pallas kernels, edge_pack(): pl.pallas_call(edge_pack_kernel, out_shape=tuple((jax.ShapeDtypeStruct(sh...  5.09 us
    all_to_all x1, waiting for transfers between devices, exchange(): lax.all_to_all(packed, ('xline', 'inline'), split_axis=0, concat_axis=0,...  3.74 us
    pallas_call x1, Pallas kernels, corner_pack(): pl.pallas_call(corner_pack_kernel, out_shape=(out, out), in_specs=[ANY] *...  1.91 us
  transfers between devices with their start and end apart: 7, of which 1 were waited for; matrix products, arithmetic and copies ran while one was open for 2% of the time, Pallas kernels for 10%

commit v1 on v0

--- a/solution.py
+++ b/solution.py
@@ -76,7 +76,7 @@
 
 def edge_pack_kernel(
     p, vi, vx, vd, m, b, low_out, high_out, near_out, far_out,
-    strips, low, high, down, up, vel, col_sems, sems, out_sems,
+    strips, low, high, down, up, vel, outer, col_sems, sems, out_sems,
 ):
     planes, columns, depth = p.shape
     col_copies = []
@@ -94,47 +94,64 @@
         (vi, planes - 4, 4, vel.at[3]),
         (vx, planes - 4, 4, vel.at[4]),
         (vd, planes - 4, 4, vel.at[5]),
-        (p, 0, 4, down.at[pl.ds(0, 4)]),
-        (m, 0, 3, down.at[pl.ds(7, 3)]),
-        (b, 0, 3, down.at[pl.ds(10, 3)]),
-        (p, planes - 4, 4, up.at[pl.ds(0, 4)]),
-        (m, planes - 3, 3, up.at[pl.ds(7, 3)]),
-        (b, planes - 4, 4, up.at[pl.ds(10, 4)]),
-        (vi, planes - 1, 1, up.at[pl.ds(14, 1)]),
+        (p, 0, 3, down.at[pl.ds(0, 3)]),
+        (m, 0, 3, down.at[pl.ds(6, 3)]),
+        (b, 0, 3, down.at[pl.ds(9, 3)]),
+        (p, planes - 3, 3, up.at[pl.ds(0, 3)]),
+        (m, planes - 3, 3, up.at[pl.ds(6, 3)]),
+        (b, planes - 3, 3, up.at[pl.ds(9, 3)]),
+        (vi, planes - 1, 1, up.at[pl.ds(12, 1)]),
+        (p, 3, 1, outer.at[pl.ds(0, 1)]),
+        (p, planes - 4, 1, outer.at[pl.ds(1, 1)]),
+        (b, planes - 4, 1, outer.at[pl.ds(2, 1)]),
     )
     copies = [
         pltpu.make_async_copy(ref.at[pl.ds(start, count)], target, sems.at[index])
         for index, (ref, start, count, target) in enumerate(jobs)
     ]
     run_copies(col_copies + copies)
-    upper = iota((8, depth), 0) >= 4
-    first = iota((8, depth), 0) == 0
-    down[14:16] = jnp.zeros((2, columns, depth), F32)
+    sub = iota((8, depth), 0)
+    down[13] = jnp.zeros((columns, depth), F32)
     for copy in col_copies:
         copy.wait()
 
-    def plane(index, _):
-        before = jnp.maximum(index - 1, 0)
-        keep = jnp.where(index > 0, 1.0, 0.0)
-        for side in range(2):
-            svi, svx, svd, sp, sm, sb = (strips.at[side, field] for field in range(6))
-            div = (
-                (svi[index] - keep * svi[before])
-                + (svx[index] - row_before(svx[index]))
-                + (svd[index] - lane_before(svd[index]))
-            )
-            turned_div = half_turn(div)
-            turned_b = half_turn(sb[index])
-            if side == 0:
-                low[index, 0:8, :] = jnp.where(upper, turned_div, sp[index])
-                low[index, 8:16, :] = jnp.where(upper, turned_b, sm[index])
-            else:
-                edge = jnp.where(first, pltpu.roll(svx[index], 1, 0), turned_div)
-                high[index, 0:8, :] = jnp.where(upper, sp[index], edge)
-                high[index, 8:16, :] = jnp.where(upper, sm[index], turned_b)
+    def pair(number, _):
+        base = pl.multiple_of(number * 24, 8)
+        shared = [[], []]
+        for half in range(2):
+            index = number * 2 + half
+            before = jnp.maximum(index - 1, 0)
+            keep = jnp.where(index > 0, 1.0, 0.0)
+            for side in range(2):
+                svi, svx, svd, sp, sm, sb = (strips.at[side, field] for field in range(6))
+                now_p, now_m, now_b = sp[index], sm[index], sb[index]
+                div = (
+                    (svi[index] - keep * svi[before])
+                    + (svx[index] - row_before(svx[index]))
+                    + (svd[index] - lane_before(svd[index]))
+                )
+                flux = COURANT * now_b * (pltpu.roll(now_p, 7, 0) - now_p)
+                if side == 0:
+                    div = jnp.where(sub == 2, div - flux, div)
+                    tile = jnp.where(
+                        sub < 3, now_p, jnp.where(sub < 6, pltpu.roll(div, 3, 0), pltpu.roll(now_m, 6, 0))
+                    )
+                    low[pl.ds(base + half * 8, 8), :] = tile
+                    rest = jnp.where(sub < 1, pltpu.roll(now_m, 6, 0), pltpu.roll(now_b, 1, 0))
+                else:
+                    div = jnp.where(sub == 5, div + pltpu.roll(flux, 1, 0), div)
+                    tile = jnp.where(
+                        sub < 3, pltpu.roll(div, 3, 0), jnp.where(sub < 5, pltpu.roll(now_m, 5, 0), now_p)
+                    )
+                    high[pl.ds(base + half * 8, 8), :] = tile
+                    rest = jnp.where(sub < 1, pltpu.roll(now_m, 3, 0), pltpu.roll(now_b, 4, 0))
+                    high[pl.ds(planes * 12 + index, 1), :] = svx[index, 7:8, :]
+                shared[side].append(rest)
+        for out, (even, odd) in zip((low, high), shared):
+            out[pl.ds(base + 16, 8), :] = jnp.where(sub < 4, even, half_turn(odd))
         return 0
 
-    lax.fori_loop(0, planes, plane, 0, unroll=8)
+    lax.fori_loop(0, planes // 2, pair, 0, unroll=4)
     outs = run_copies(
         [
             pltpu.make_async_copy(low, low_out, out_sems.at[0]),
@@ -144,17 +161,19 @@
     for copy in copies[:6]:
         copy.wait()
     last = columns - 1
-    for base, out, line in ((0, down, 13), (3, up, 15)):
+    for base, out, line in ((0, down, 12), (3, up, 13)):
         for step in range(1, 4):
             div_i = vel[base, step]
             if base or step > 1:
                 div_i = div_i - vel[base, step - 1]
             vx_now = vel[base + 1, step]
             vd_now = vel[base + 2, step]
-            out[3 + step] = div_i + (vx_now - row_before(vx_now)) + (vd_now - lane_before(vd_now))
+            out[2 + step] = div_i + (vx_now - row_before(vx_now)) + (vd_now - lane_before(vd_now))
             out[line, step - 1 : step, :] = vel[base + 1, step, last : last + 1, :]
     for copy in copies[6:]:
         copy.wait()
+    down[5] = down[5] - COURANT * down[11] * (outer[0] - down[2])
+    up[3] = up[3] + COURANT * outer[2] * (up[0] - outer[1])
     even = lax.axis_index("inline") % 2 == 0
     outs.append(Either(even, up, down, (), near_out, out_sems.at[2]))
     outs.append(Either(even, down, up, (), far_out, out_sems.at[3]))
@@ -165,22 +184,24 @@
 
 def edge_pack(p, vi, vx, vd, m, b):
     planes, columns, depth = p.shape
-    cols = (planes, 16, depth)
-    sheets = (16, columns, depth)
+    low = (planes * 12, depth)
+    high = (planes * 13, depth)
+    sheets = (14, columns, depth)
     return pl.pallas_call(
         edge_pack_kernel,
-        out_shape=tuple(jax.ShapeDtypeStruct(shape, F32) for shape in (cols, cols, sheets, sheets)),
+        out_shape=tuple(jax.ShapeDtypeStruct(shape, F32) for shape in (low, high, sheets, sheets)),
         in_specs=[ANY] * 6,
         out_specs=(ANY,) * 4,
         scratch_shapes=[
             pltpu.VMEM((2, 6, planes, 8, depth), F32),
-            pltpu.VMEM(cols, F32),
-            pltpu.VMEM(cols, F32),
+            pltpu.VMEM(low, F32),
+            pltpu.VMEM(high, F32),
             pltpu.VMEM(sheets, F32),
             pltpu.VMEM(sheets, F32),
             pltpu.VMEM((6, 4, columns, depth), F32),
+            pltpu.VMEM((3, columns, depth), F32),
             pltpu.SemaphoreType.DMA((2, 6)),
-            pltpu.SemaphoreType.DMA((13,)),
+            pltpu.SemaphoreType.DMA((16,)),
             pltpu.SemaphoreType.DMA((4,)),
         ],
         compiler_params=pltpu.CompilerParams(vmem_limit_bytes=VMEM_LIMIT),
@@ -209,16 +230,16 @@
     for side, start in ((0, 0), (1, columns - 8)):
         window = pl.ds(start, 8)
         copies += [
-            Either(even, near, far, (pl.ds(0, 13), window), dn.at[side], sems.at[side, 0]),
-            Either(even, far, near, (pl.ds(0, 15), window), upv.at[side], sems.at[side, 1]),
+            Either(even, near, far, (pl.ds(0, 12), window), dn.at[side], sems.at[side, 0]),
+            Either(even, far, near, (pl.ds(0, 13), window), upv.at[side], sems.at[side, 1]),
             pltpu.make_async_copy(vi.at[planes - 1, window, :], vi_last.at[side], sems.at[side, 2]),
             pltpu.make_async_copy(
-                (low_cols, high_cols)[side].at[0, pl.ds(0, 8), :], row0.at[side], sems.at[side, 3]
+                (low_cols, high_cols)[side].at[pl.ds(0, 8), :], row0.at[side], sems.at[side, 3]
             ),
         ]
     lines = [
-        Either(even, far, near, (15, pl.ds(0, 8)), dn.at[2, 0], sems.at[2, 0]),
-        Either(even, near, far, (13, pl.ds(0, 8)), dn.at[2, 1], sems.at[2, 1]),
+        Either(even, far, near, (13, pl.ds(0, 8)), dn.at[2, 0], sems.at[2, 0]),
+        Either(even, near, far, (12, pl.ds(0, 8)), dn.at[2, 1], sems.at[2, 1]),
     ]
     run_copies(copies + lines)
     for copy in copies + lines:
@@ -230,18 +251,18 @@
             col = dj - 1 if side == 0 else 8 - dj
             at = slice(col, col + 1)
             if kind == "first":
-                place = 3 + dj if side == 0 else 4 - dj
+                place = 2 + dj if side == 0 else 3 - dj
                 value = row0[side, place : place + 1, :]
-                value = value - jnp.where(has_before, upv[side, 14, at, :], 0.0)
+                value = value - jnp.where(has_before, upv[side, 12, at, :], 0.0)
             elif kind == "line":
                 line = di - 1 if z else 3 - di
                 value = dn[2, z, line : line + 1, :]
             elif z:
-                value = dn[side, {"p": 0, "d": 4, "m": 7, "b": 10}[kind] + di - 1, at, :]
+                value = dn[side, {"p": 0, "d": 3, "m": 6, "b": 9}[kind] + di - 1, at, :]
                 if kind == "d" and di == 1:
                     value = value - vi_last[side, at, :]
             else:
-                value = upv[side, {"p": 4, "d": 7, "m": 10, "b": 14}[kind] - di, at, :]
+                value = upv[side, {"p": 3, "d": 6, "m": 9, "b": 12}[kind] - di, at, :]
             out[row : row + 1, :] = value
 
 
@@ -254,8 +275,8 @@
         in_specs=[ANY] * 5,
         out_specs=(VMEM, VMEM),
         scratch_shapes=[
-            pltpu.VMEM((3, 13, 8, depth), F32),
-            pltpu.VMEM((2, 15, 8, depth), F32),
+            pltpu.VMEM((3, 12, 8, depth), F32),
+            pltpu.VMEM((2, 13, 8, depth), F32),
             pltpu.VMEM((2, 8, depth), F32),
             pltpu.VMEM((2, 8, depth), F32),
             pltpu.SemaphoreType.DMA((3, 4)),
@@ -372,19 +393,19 @@
         (corner_l, cor_l),
     )
     up_jobs = (
-        (pl.ds(0, 4), pb.at[0, pl.ds(0, 4), own_c, :]),
-        (pl.ds(4, 3), div.at[pl.ds(1, 3), own_c, :]),
-        (pl.ds(7, 3), mb.at[pl.ds(1, 3), own_c, :]),
-        (pl.ds(10, 4), bb.at[pl.ds(0, 4), own_c, :]),
-        (14, v0.at[0]),
-        ((15, pl.ds(0, 8)), lines.at[0]),
+        (pl.ds(0, 3), pb.at[0, pl.ds(1, 3), own_c, :]),
+        (pl.ds(3, 3), div.at[pl.ds(1, 3), own_c, :]),
+        (pl.ds(6, 3), mb.at[pl.ds(1, 3), own_c, :]),
+        (pl.ds(9, 3), bb.at[pl.ds(1, 3), own_c, :]),
+        (12, v0.at[0]),
+        ((13, pl.ds(0, 8)), lines.at[0]),
     )
     down_jobs = (
-        (pl.ds(0, 4), pb.at[0, pl.ds(planes + 4, 4), own_c, :]),
-        (pl.ds(4, 3), div.at[pl.ds(planes + 4, 3), own_c, :]),
-        (pl.ds(7, 3), mb.at[pl.ds(planes + 4, 3), own_c, :]),
-        (pl.ds(10, 3), bb.at[pl.ds(planes + 4, 3), own_c, :]),
-        ((13, pl.ds(0, 8)), lines.at[1]),
+        (pl.ds(0, 3), pb.at[0, pl.ds(planes + 4, 3), own_c, :]),
+        (pl.ds(3, 3), div.at[pl.ds(planes + 4, 3), own_c, :]),
+        (pl.ds(6, 3), mb.at[pl.ds(planes + 4, 3), own_c, :]),
+        (pl.ds(9, 3), bb.at[pl.ds(planes + 4, 3), own_c, :]),
+        ((12, pl.ds(0, 8)), lines.at[1]),
     )
     even = at_i % 2 == 0
     copies = [pltpu.make_async_copy(src, dst, sems.at[index]) for index, (src, dst) in enumerate(jobs)]
@@ -415,22 +436,33 @@
     top = iota((8, depth), 0) == 0
     top_own = iota((columns, depth), 0) == 0
     edge = slice(columns, columns + 8)
-    upper = iota((8, depth), 0) >= 4
+    sub_d = iota((8, depth), 0)
+    upper = sub_d >= 4
     square = COURANT * COURANT
 
     def own_plane(index):
         plane = index + 4
-        a_l, b_l = strip_l[index, 0:8, :], strip_l[index, 8:16, :]
-        a_r, b_r = strip_r[index, 0:8, :], strip_r[index, 8:16, :]
+        pair, odd = index // 2, index % 2
+        tile_at = pl.ds(pl.multiple_of(pair * 24 + odd * 8, 8), 8)
+        rest_at = pl.ds(pl.multiple_of(pair * 24 + 16, 8), 8)
+        t_l, t_r = strip_l[tile_at, :], strip_r[tile_at, :]
+        rest_l, rest_r = strip_l[rest_at, :], strip_r[rest_at, :]
+        rest_l = jnp.where(odd == 1, half_turn(rest_l), rest_l)
+        rest_r = jnp.where(odd == 1, half_turn(rest_r), rest_r)
+        vx_l = keep_x * strip_l[pl.ds(planes * 12 + index, 1), :]
         now_x, now_d = v1[index], v2[index]
-        pb[0, plane, edge, :] = jnp.where(upper, a_l, end_x * a_r)
-        mb[plane, edge, :] = jnp.where(upper, b_l, end_x * b_r)
-        turned = half_turn(jnp.where(upper, a_r, a_l))
+        p_l = jnp.where(sub_d == 4, pltpu.roll(t_l, 7, 0), t_l)
+        p_r = jnp.where(sub_d == 3, pltpu.roll(t_r, 1, 0), t_r)
+        pb[0, plane, edge, :] = jnp.where(upper, p_l, end_x * p_r)
+        m_l = jnp.where(sub_d == 5, pltpu.roll(rest_l, 5, 0), pltpu.roll(t_l, 3, 0))
+        m_r = jnp.where(sub_d == 2, pltpu.roll(rest_r, 2, 0), pltpu.roll(t_r, 2, 0))
+        mb[plane, edge, :] = jnp.where(upper, m_l, end_x * m_r)
+        turned = pltpu.roll(jnp.where((sub_d >= 3) & (sub_d < 6), t_r, t_l), 5, 0)
         div[plane, edge, :] = COURANT * (turned - jnp.where(top, now_x[columns - 1 : columns, :], 0.0))
-        buoy = square * half_turn(jnp.where(upper, b_r, keep_x * b_l))
+        buoy = square * jnp.where(upper, keep_x * half_turn(rest_l), pltpu.roll(rest_r, 7, 0))
         bs[plane, edge, :] = buoy
         bk[plane, edge, :] = lane_before(buoy)
-        x_before = jnp.where(top_own, keep_x * a_l[0:1, :], pltpu.roll(now_x, 1, 0))
+        x_before = jnp.where(top_own, vx_l, pltpu.roll(now_x, 1, 0))
         div[plane, own_c, :] = COURANT * (
             (v0[index + 1] - v0[index]) + (now_x - x_before) + (now_d - lane_before(now_d))
         )
@@ -575,6 +607,9 @@
     for copy in late:
         copy.wait()
 
+    bb[0] = jnp.zeros((rows, depth), F32)
+    pb[0, 0, own_c, :] = pb[0, 1, own_c, :]
+    pb[0, planes + 7, own_c, :] = pb[0, planes + 6, own_c, :]
     own_line = v1[0, columns - 1 : columns, :]
     for side, box in ((0, cor_r), (1, cor_l)):
         for row, (kind, z, di, dj) in enumerate(corner_rows(side)):
@@ -720,8 +755,8 @@
             pltpu.VMEM(block, F32),
             pltpu.VMEM(full, F32),
             pltpu.VMEM((2, 8, depth), F32),
-            pltpu.VMEM((planes, 16, depth), F32),
-            pltpu.VMEM((planes, 16, depth), F32),
+            pltpu.VMEM((planes * 12, depth), F32),
+            pltpu.VMEM((planes * 13, depth), F32),
             pltpu.VMEM((CORNER_ROWS, depth), F32),
             pltpu.VMEM((CORNER_ROWS, depth), F32),
             pltpu.VMEM((devices * 8 + 8, SLOTS), F32),

time: 75.5 us -> 72.6 us (0.962)
  starting transfers between devices: 22.1 us -> 20 us
    ppermute x1, starting transfers between devices: 9.44 us -> 8.29 us  [shards(): lax.ppermute(far_send, 'inline', [(source, source if source in (0, count...]
    all_to_all x1, starting transfers between devices: 5.98 us -> 5.08 us  [exchange(): lax.all_to_all(packed, ('xline', 'inline'), split_axis=0, concat_axis=0,...]
  transfers between devices with their start and end apart: 7 -> 7, of which waited for: 1 -> 1; matrix products, arithmetic and copies ran while one was open for 2% -> 2% of each run, Pallas kernels for 10% -> 11%
where the time goes in v1:
time: 72.6 us; the launch traced here: 71.6 us
  Pallas kernels  44.5 us (61%)
  starting transfers between devices  20 us (28%)
  waiting for transfers between devices  3.6 us (5%)
  other arithmetic  1.6 us (2%)
  between operations  1.56 us (2%)
    pallas_call x1, Pallas kernels, step_all(): pl.pallas_call(functools.partial(step_kernel, 0 if more is None else more...  32 us
    ppermute x1, starting transfers between devices, shards(): lax.ppermute(far_send, 'inline', [(source, source if source in (0, count...  8.29 us
    ppermute x4, starting transfers between devices, rotate(): lax.ppermute(value, axis, [(source, (source + steps) % count) for source...  6.12 us
    pallas_call x1, Pallas kernels, route(): pl.pallas_call(functools.partial(route_kernel, rounds, n_inline, n_xline,...  5.63 us
    all_to_all x1, starting transfers between devices, exchange(): lax.all_to_all(packed, ('xline', 'inline'), split_axis=0, concat_axis=0,...  5.08 us
    pallas_call x1, Pallas kernels, edge_pack(): pl.pallas_call(edge_pack_kernel, out_shape=tuple((jax.ShapeDtypeStruct(sh...  5.03 us
    all_to_all x1, waiting for transfers between devices, exchange(): lax.all_to_all(packed, ('xline', 'inline'), split_axis=0, concat_axis=0,...  3.58 us
    pallas_call x1, Pallas kernels, corner_pack(): pl.pallas_call(corner_pack_kernel, out_shape=(out, out), in_specs=[ANY] *...  1.89 us
  transfers between devices with their start and end apart: 7, of which 1 were waited for; matrix products, arithmetic and copies ran while one was open for 2% of the time, Pallas kernels for 11%

profile of v1, /device:TPU:0, one launch (start us, length us, event | category | flops | bytes accessed | tf_op | source)
XLA Modules:
  0.0 71.6 jit_solution(10224727434349933788)
XLA Ops:
  0.6 5.0 %shard_map.138 = (f32[384,256]{1,0:T(8,128)}, f32[416,256]{1,0:T(8,128)}, f32[14,64,256]{2,1,0:T(8,128)}, f32[14,64,256]{2,1,0:T(8,128)}) custom-call(f32[32,64,256]{2,1,0:T(8,128)} %p.1, f32[32,64,256]{2,1,0:T(8,128)} %vi.3, f32[32,64,256]{2,1,0:T(8,128)} %vx.1, f32[32,64,256]{2,1,0:T(8,128)} %vd.1, f32[32,64,256]{2,1,0:T(8,128)} %m.1, f32[32,64,256]{2,1,0:T(8,128)} %b.1), custom_call_target="tpu_custom_call" | custom-call | tf_op jit(solution)/shard_map/pallas_call | solution.py:190
  5.7 0.5 collective-permute-start
  6.2 8.3 %collective-permute-start.1 = (f32[14,64,256]{2,1,0:T(8,128)}, f32[14,64,256]{2,1,0:T(8,128)}, u32[]{:S(2)}, u32[]{:S(2)}) collective-permute-start(f32[14,64,256]{2,1,0:T(8,128)} %get-tuple-element.101), channel_id=1, source_target_pairs={{0,0},{1,2},{2,1},{3,4},{4,3},{5,6},{6,5},{7,7},{8,8},{9,10},{10,9... | collective-permute-start | bytes 2752520 | tf_op jit(solution)/shard_map/ppermute | solution.py:794
  14.5 2.5 %collective-permute-start.3 = (f32[416,256]{1,0:T(8,128)}, f32[416,256]{1,0:T(8,128)}, u32[]{:S(2)}, u32[]{:S(2)}) collective-permute-start(f32[416,256]{1,0:T(8,128)} %get-tuple-element.103.high_cols), channel_id=1, source_target_pairs={{0,8},{8,16},{16,24},{24,0},{1,9},{9,17},{17,25},{25,1},{2,10},{10... | collective-permute-start | bytes 1277960 | tf_op jit(solution)/shard_map/ppermute | solution.py:31
  17.0 1.0 %collective-permute-start.2 = (f32[384,256]{1,0:T(8,128)}, f32[384,256]{1,0:T(8,128)}, u32[]{:S(2)}, u32[]{:S(2)}) collective-permute-start(f32[384,256]{1,0:T(8,128)} %get-tuple-element.102.low_cols), channel_id=1, source_target_pairs={{0,24},{8,0},{16,8},{24,16},{1,25},{9,1},{17,9},{25,17},{2,26},{10... | collective-permute-start | bytes 1179656 | tf_op jit(solution)/shard_map/ppermute | solution.py:31
  17.9 5.6 %shard_map.137 = f32[256,128]{1,0:T(8,128)} custom-call(f32[768,512]{1,0:T(8,128)} %traces.1, f32[4,512]{1,0:T(4,128)} %resample.1, s32[1,768]{1,0:T(1,128)} %bitcast.20, s32[768]{0:T(1024)} %cell.1), custom_call_target="tpu_custom_call" | custom-call | tf_op jit(solution)/shard_map/pallas_call | solution.py:350
  23.6 5.1 %all-to-all-start.4 = ((f32[32,8,128]{2,1,0:T(8,128)}), f32[32,8,128]{2,1,0:T(8,128)}, u32[]{:S(2)}, u32[]{:S(2)}) async-start(f32[32,8,128]{2,1,0:T(8,128)} %bitcast.15), calls=%async_computation.4 | async-start | bytes 262144 | tf_op jit(solution)/shard_map/all_to_all | solution.py:804
  28.7 0.0 collective-permute-done.near
  28.7 0.0 collective-permute-done.1.far
  28.7 1.9 %shard_map.139 = (f32[48,256]{1,0:T(8,128)}, f32[48,256]{1,0:T(8,128)}) custom-call(f32[14,64,256]{2,1,0:T(8,128)} %collective-permute-done.near, f32[14,64,256]{2,1,0:T(8,128)} %collective-permute-done.1.far, f32[384,256]{1,0:T(8,128)} %get-tuple-element.102.low_cols, f32[416,256]{1,0:T(8,128)} %get-tuple-element.103.high_cols, f32[32,64,256]{2,1,0:T(8,128)} %vi.3), custom_call_target="tpu_custom_call" | custom-call | tf_op jit(solution)/shard_map/pallas_call | solution.py:272
  30.6 2.6 %collective-permute-start.4 = (f32[48,256]{1,0:T(8,128)}, f32[48,256]{1,0:T(8,128)}, u32[]{:S(2)}, u32[]{:S(2)}) collective-permute-start(f32[48,256]{1,0:T(8,128)} %get-tuple-element.104), channel_id=1, source_target_pairs={{0,24},{8,0},{16,8},{24,16},{1,25},{9,1},{17,9},{25,17},{2,26},{10... | collective-permute-start | bytes 147464 | tf_op jit(solution)/shard_map/ppermute | solution.py:31
  33.2 0.0 collective-permute-start.5
  33.2 3.6 %all-to-all-done.4 = f32[32,8,128]{2,1,0:T(8,128)} async-done(((f32[32,8,128]{2,1,0:T(8,128)}), f32[32,8,128]{2,1,0:T(8,128)}, u32[]{:S(2)}, u32[]{:S(2)}) %all-to-all-start.4) | async-done | bytes 131104 | tf_op jit(solution)/shard_map/all_to_all | solution.py:804
  36.8 1.6 %reduce_max.9 = f32[]{:T(128)} reduce(f32[32,8,128]{2,1,0:T(8,128)} %all-to-all-done.4, f32[]{:T(128)} %constant.0.clone.1), dimensions={0,1,2}, to_apply=%region_0.0 | reduce | flops 32767 | bytes 131080 | tf_op jit(solution)/shard_map/reduce_max | solution.py:810
  39.1 0.0 collective-permute-done.2
  39.1 0.0 collective-permute-done.3
  39.1 0.0 collective-permute-done.4
  39.1 0.0 collective-permute-done.5
  39.1 32.2 %conditional.1 = ((f32[32,64,256]{2,1,0:T(8,128)}, f32[32,64,256]{2,1,0:T(8,128)}, f32[32,64,256]{2,1,0:T(8,128)}, f32[32,64,256]{2,1,0:T(8,128)})) conditional(s32[]{:T(128)} %convert_element_type.3, (f32[256,128]{1,0:T(8,128)}, f32[32,64,256]{2,1,0:T(8,128)}, f32[32,64,256]{2,1,0:T(8,128)}, f32[32,64,256]{2,1,0:T(8,128)}, f32[32,64,256]{2,1,0:T(8,128)}, ...), branch_computations={%region_1.0_spmd, %region_2.0_spmd} | conditional | flops 393216 | bytes 3145736 | solution.py:822
  39.2 32.0 %branch_0_fun.1 = (f32[32,64,256]{2,1,0:T(8,128)}, f32[32,64,256]{2,1,0:T(8,128)}, f32[32,64,256]{2,1,0:T(8,128)}, f32[32,64,256]{2,1,0:T(8,128)}) custom-call(f32[256,128]{1,0:T(8,128)} %get-tuple-element.60.refs_0_, f32[32,64,256]{2,1,0:T(8,128)} %get-tuple-element.61.refs_1_, f32[32,64,256]{2,1,0:T(8,128)} %get-tuple-element.62.refs_2_, ...), custom_call_target="tpu_custom_call" | custom-call | tf_op jit(solution)/shard_map/cond/branch_0_fun/pallas_call | solution.py:741
Async XLA Ops:
  5.7 23.0 %collective-permute-start = (f32[14,64,256]{2,1,0:T(8,128)}, f32[14,64,256]{2,1,0:T(8,128)}, u32[]{:S(2)}, u32[]{:S(2)}) collective-permute-start(f32[14,64,256]{2,1,0:T(8,128)} %get-tuple-element.100), channel_id=1, source_target_pairs={{0,1},{1,0},{2,3},{3,2},{4,5},{5,4},{6,7},{7,6},{8,9},{9,8},{10,11... | collective-permute-start | bytes 2752520 | tf_op jit(solution)/shard_map/ppermute | solution.py:793
  6.2 22.5 %collective-permute-start.1 = (f32[14,64,256]{2,1,0:T(8,128)}, f32[14,64,256]{2,1,0:T(8,128)}, u32[]{:S(2)}, u32[]{:S(2)}) collective-permute-start(f32[14,64,256]{2,1,0:T(8,128)} %get-tuple-element.101), channel_id=1, source_target_pairs={{0,0},{1,2},{2,1},{3,4},{4,3},{5,6},{6,5},{7,7},{8,8},{9,10},{10,9... | collective-permute-start | bytes 2752520 | tf_op jit(solution)/shard_map/ppermute | solution.py:794
  14.5 24.6 %collective-permute-start.3 = (f32[416,256]{1,0:T(8,128)}, f32[416,256]{1,0:T(8,128)}, u32[]{:S(2)}, u32[]{:S(2)}) collective-permute-start(f32[416,256]{1,0:T(8,128)} %get-tuple-element.103.high_cols), channel_id=1, source_target_pairs={{0,8},{8,16},{16,24},{24,0},{1,9},{9,17},{17,25},{25,1},{2,10},{10... | collective-permute-start | bytes 1277960 | tf_op jit(solution)/shard_map/ppermute | solution.py:31
  17.0 22.1 %collective-permute-start.2 = (f32[384,256]{1,0:T(8,128)}, f32[384,256]{1,0:T(8,128)}, u32[]{:S(2)}, u32[]{:S(2)}) collective-permute-start(f32[384,256]{1,0:T(8,128)} %get-tuple-element.102.low_cols), channel_id=1, source_target_pairs={{0,24},{8,0},{16,8},{24,16},{1,25},{9,1},{17,9},{25,17},{2,26},{10... | collective-permute-start | bytes 1179656 | tf_op jit(solution)/shard_map/ppermute | solution.py:31
  23.6 13.2 %all-to-all-start.4 = ((f32[32,8,128]{2,1,0:T(8,128)}), f32[32,8,128]{2,1,0:T(8,128)}, u32[]{:S(2)}, u32[]{:S(2)}) async-start(f32[32,8,128]{2,1,0:T(8,128)} %bitcast.15), calls=%async_computation.4 | async-start | bytes 262144 | tf_op jit(solution)/shard_map/all_to_all | solution.py:804
  30.6 8.5 %collective-permute-start.4 = (f32[48,256]{1,0:T(8,128)}, f32[48,256]{1,0:T(8,128)}, u32[]{:S(2)}, u32[]{:S(2)}) collective-permute-start(f32[48,256]{1,0:T(8,128)} %get-tuple-element.104), channel_id=1, source_target_pairs={{0,24},{8,0},{16,8},{24,16},{1,25},{9,1},{17,9},{25,17},{2,26},{10... | collective-permute-start | bytes 147464 | tf_op jit(solution)/shard_map/ppermute | solution.py:31
  33.2 5.9 %collective-permute-start.5 = (f32[48,256]{1,0:T(8,128)}, f32[48,256]{1,0:T(8,128)}, u32[]{:S(2)}, u32[]{:S(2)}) collective-permute-start(f32[48,256]{1,0:T(8,128)} %get-tuple-element.105), channel_id=1, source_target_pairs={{0,8},{8,16},{16,24},{24,0},{1,9},{9,17},{17,25},{25,1},{2,10},{10... | collective-permute-start | bytes 147464 | tf_op jit(solution)/shard_map/ppermute | solution.py:31

commit v2 on v1

--- a/solution.py
+++ b/solution.py
@@ -115,6 +115,21 @@
     for copy in col_copies:
         copy.wait()
 
+    for copy in copies[6:]:
+        copy.wait()
+    even = lax.axis_index("inline") % 2 == 0
+
+    def leave(part, start, size):
+        window = pl.ds(start, size)
+        return run_copies(
+            [
+                Either(even, up, down, window, near_out.at[window], out_sems.at[part, 0]),
+                Either(even, down, up, window, far_out.at[window], out_sems.at[part, 1]),
+            ]
+        )
+
+    outs = leave(0, 0, 3) + leave(1, 6, 6)
+
     def pair(number, _):
         base = pl.multiple_of(number * 24, 8)
         shared = [[], []]
@@ -152,10 +167,10 @@
         return 0
 
     lax.fori_loop(0, planes // 2, pair, 0, unroll=4)
-    outs = run_copies(
+    outs += run_copies(
         [
-            pltpu.make_async_copy(low, low_out, out_sems.at[0]),
-            pltpu.make_async_copy(high, high_out, out_sems.at[1]),
+            pltpu.make_async_copy(low, low_out, out_sems.at[4, 0]),
+            pltpu.make_async_copy(high, high_out, out_sems.at[4, 1]),
         ]
     )
     for copy in copies[:6]:
@@ -170,14 +185,9 @@
             vd_now = vel[base + 2, step]
             out[2 + step] = div_i + (vx_now - row_before(vx_now)) + (vd_now - lane_before(vd_now))
             out[line, step - 1 : step, :] = vel[base + 1, step, last : last + 1, :]
-    for copy in copies[6:]:
-        copy.wait()
     down[5] = down[5] - COURANT * down[11] * (outer[0] - down[2])
     up[3] = up[3] + COURANT * outer[2] * (up[0] - outer[1])
-    even = lax.axis_index("inline") % 2 == 0
-    outs.append(Either(even, up, down, (), near_out, out_sems.at[2]))
-    outs.append(Either(even, down, up, (), far_out, out_sems.at[3]))
-    run_copies(outs[2:])
+    outs += leave(2, 3, 3) + leave(3, 12, 2)
     for copy in outs:
         copy.wait()
 
@@ -202,7 +212,7 @@
             pltpu.VMEM((3, columns, depth), F32),
             pltpu.SemaphoreType.DMA((2, 6)),
             pltpu.SemaphoreType.DMA((16,)),
-            pltpu.SemaphoreType.DMA((4,)),
+            pltpu.SemaphoreType.DMA((5, 2)),
         ],
         compiler_params=pltpu.CompilerParams(vmem_limit_bytes=VMEM_LIMIT),
     )(p, vi, vx, vd, m, b)
@@ -562,19 +572,27 @@
             rows_at = [pl.ds(pl.multiple_of((code >> 7) * 8, 8), 8) for code in found]
             return [spread(values, code, base + unit) for unit, code in enumerate(found)], rows_at
 
-        def batch(index, _):
+        def add_groups(index):
             ready = [prepare(index * GROUPS + group) for group in range(GROUPS)]
             for adds, rows_at in ready:
                 sums = [inj[row, :] + add for row, add in zip(rows_at, adds)]
                 for row, value in zip(rows_at, sums):
                     inj[row, :] = value
-            own_plane(jnp.minimum(index, planes - 1))
+
+        def both(index, _):
+            add_groups(index)
+            own_plane(index)
+            return 0
+
+        def batch(index, _):
+            add_groups(index)
             return 0
 
         if not rounds:
             start_block()
         turns = jnp.maximum((total + GROUPS - 1) // GROUPS, planes)
-        lax.fori_loop(0, turns, batch, 0)
+        lax.fori_loop(0, planes, both, 0)
+        lax.fori_loop(planes, turns, batch, 0)
 
         def put_off_list(source, _):
             @pl.when(counts[source, 2] > 0)

time: 72.6 us -> 74 us (1.019); the launches traced: 71.6 us -> 74.5 us
  Pallas kernels: 44.5 us -> 47.5 us
    pallas_call x1, Pallas kernels: 32 us -> 35.2 us  [step_all(): pl.pallas_call(functools.partial(step_kernel, 0 if more is None else more...]
  transfers between devices with their start and end apart: 7 -> 7, of which waited for: 1 -> 1; matrix products, arithmetic and copies ran while one was open for 2% -> 2% of each run, Pallas kernels for 11% -> 10%
where the time goes in v2:
time: 74 us; the launch traced here: 74.5 us
  Pallas kernels  47.5 us (64%)
  starting transfers between devices  20 us (27%)
  waiting for transfers between devices  3.6 us (5%)
  other arithmetic  1.6 us (2%)
  between operations  1.56 us (2%)
    pallas_call x1, Pallas kernels, step_all(): pl.pallas_call(functools.partial(step_kernel, 0 if more is None else more...  35.2 us
    ppermute x1, starting transfers between devices, shards(): lax.ppermute(far_send, 'inline', [(source, source if source in (0, count...  8.29 us
    ppermute x4, starting transfers between devices, rotate(): lax.ppermute(value, axis, [(source, (source + steps) % count) for source...  6.12 us
    pallas_call x1, Pallas kernels, route(): pl.pallas_call(functools.partial(route_kernel, rounds, n_inline, n_xline,...  5.63 us
    all_to_all x1, starting transfers between devices, exchange(): lax.all_to_all(packed, ('xline', 'inline'), split_axis=0, concat_axis=0,...  5.08 us
    pallas_call x1, Pallas kernels, edge_pack(): pl.pallas_call(edge_pack_kernel, out_shape=tuple((jax.ShapeDtypeStruct(sh...  4.71 us
    all_to_all x1, waiting for transfers between devices, exchange(): lax.all_to_all(packed, ('xline', 'inline'), split_axis=0, concat_axis=0,...  3.58 us
    pallas_call x1, Pallas kernels, corner_pack(): pl.pallas_call(corner_pack_kernel, out_shape=(out, out), in_specs=[ANY] *...  1.89 us
  transfers between devices with their start and end apart: 7, of which 1 were waited for; matrix products, arithmetic and copies ran while one was open for 2% of the time, Pallas kernels for 10%

profile of v2, /device:TPU:0, one launch (start us, length us, event | category | flops | bytes accessed | tf_op | source)
XLA Modules:
  0.0 74.5 jit_solution(17541476902473271130)
XLA Ops:
  0.6 4.7 %shard_map.138 = (f32[384,256]{1,0:T(8,128)}, f32[416,256]{1,0:T(8,128)}, f32[14,64,256]{2,1,0:T(8,128)}, f32[14,64,256]{2,1,0:T(8,128)}) custom-call(f32[32,64,256]{2,1,0:T(8,128)} %p.1, f32[32,64,256]{2,1,0:T(8,128)} %vi.3, f32[32,64,256]{2,1,0:T(8,128)} %vx.1, f32[32,64,256]{2,1,0:T(8,128)} %vd.1, f32[32,64,256]{2,1,0:T(8,128)} %m.1, f32[32,64,256]{2,1,0:T(8,128)} %b.1), custom_call_target="tpu_custom_call" | custom-call | tf_op jit(solution)/shard_map/pallas_call | solution.py:200
  5.3 0.5 collective-permute-start
  5.9 8.3 %collective-permute-start.1 = (f32[14,64,256]{2,1,0:T(8,128)}, f32[14,64,256]{2,1,0:T(8,128)}, u32[]{:S(2)}, u32[]{:S(2)}) collective-permute-start(f32[14,64,256]{2,1,0:T(8,128)} %get-tuple-element.101), channel_id=1, source_target_pairs={{0,0},{1,2},{2,1},{3,4},{4,3},{5,6},{6,5},{7,7},{8,8},{9,10},{10,9... | collective-permute-start | bytes 2752520 | tf_op jit(solution)/shard_map/ppermute | solution.py:812
  14.2 2.5 %collective-permute-start.3 = (f32[416,256]{1,0:T(8,128)}, f32[416,256]{1,0:T(8,128)}, u32[]{:S(2)}, u32[]{:S(2)}) collective-permute-start(f32[416,256]{1,0:T(8,128)} %get-tuple-element.103.high_cols), channel_id=1, source_target_pairs={{0,8},{8,16},{16,24},{24,0},{1,9},{9,17},{17,25},{25,1},{2,10},{10... | collective-permute-start | bytes 1277960 | tf_op jit(solution)/shard_map/ppermute | solution.py:31
  16.7 1.0 %collective-permute-start.2 = (f32[384,256]{1,0:T(8,128)}, f32[384,256]{1,0:T(8,128)}, u32[]{:S(2)}, u32[]{:S(2)}) collective-permute-start(f32[384,256]{1,0:T(8,128)} %get-tuple-element.102.low_cols), channel_id=1, source_target_pairs={{0,24},{8,0},{16,8},{24,16},{1,25},{9,1},{17,9},{25,17},{2,26},{10... | collective-permute-start | bytes 1179656 | tf_op jit(solution)/shard_map/ppermute | solution.py:31
  17.6 5.6 %shard_map.137 = f32[256,128]{1,0:T(8,128)} custom-call(f32[768,512]{1,0:T(8,128)} %traces.1, f32[4,512]{1,0:T(4,128)} %resample.1, s32[1,768]{1,0:T(1,128)} %bitcast.20, s32[768]{0:T(1024)} %cell.1), custom_call_target="tpu_custom_call" | custom-call | tf_op jit(solution)/shard_map/pallas_call | solution.py:360
  23.3 5.1 %all-to-all-start.4 = ((f32[32,8,128]{2,1,0:T(8,128)}), f32[32,8,128]{2,1,0:T(8,128)}, u32[]{:S(2)}, u32[]{:S(2)}) async-start(f32[32,8,128]{2,1,0:T(8,128)} %bitcast.15), calls=%async_computation.4 | async-start | bytes 262144 | tf_op jit(solution)/shard_map/all_to_all | solution.py:822
  28.4 0.0 collective-permute-done.near
  28.4 0.0 collective-permute-done.1.far
  28.4 1.9 %shard_map.139 = (f32[48,256]{1,0:T(8,128)}, f32[48,256]{1,0:T(8,128)}) custom-call(f32[14,64,256]{2,1,0:T(8,128)} %collective-permute-done.near, f32[14,64,256]{2,1,0:T(8,128)} %collective-permute-done.1.far, f32[384,256]{1,0:T(8,128)} %get-tuple-element.102.low_cols, f32[416,256]{1,0:T(8,128)} %get-tuple-element.103.high_cols, f32[32,64,256]{2,1,0:T(8,128)} %vi.3), custom_call_target="tpu_custom_call" | custom-call | tf_op jit(solution)/shard_map/pallas_call | solution.py:282
  30.3 2.6 %collective-permute-start.4 = (f32[48,256]{1,0:T(8,128)}, f32[48,256]{1,0:T(8,128)}, u32[]{:S(2)}, u32[]{:S(2)}) collective-permute-start(f32[48,256]{1,0:T(8,128)} %get-tuple-element.104), channel_id=1, source_target_pairs={{0,24},{8,0},{16,8},{24,16},{1,25},{9,1},{17,9},{25,17},{2,26},{10... | collective-permute-start | bytes 147464 | tf_op jit(solution)/shard_map/ppermute | solution.py:31
  32.9 0.0 collective-permute-start.5
  32.9 3.6 %all-to-all-done.4 = f32[32,8,128]{2,1,0:T(8,128)} async-done(((f32[32,8,128]{2,1,0:T(8,128)}), f32[32,8,128]{2,1,0:T(8,128)}, u32[]{:S(2)}, u32[]{:S(2)}) %all-to-all-start.4) | async-done | bytes 131104 | tf_op jit(solution)/shard_map/all_to_all | solution.py:822
  36.5 1.6 %reduce_max.9 = f32[]{:T(128)} reduce(f32[32,8,128]{2,1,0:T(8,128)} %all-to-all-done.4, f32[]{:T(128)} %constant.0.clone.1), dimensions={0,1,2}, to_apply=%region_0.0 | reduce | flops 32767 | bytes 131080 | tf_op jit(solution)/shard_map/reduce_max | solution.py:828
  38.8 0.0 collective-permute-done.2
  38.8 0.0 collective-permute-done.3
  38.8 0.0 collective-permute-done.4
  38.8 0.0 collective-permute-done.5
  38.8 35.5 %conditional.1 = ((f32[32,64,256]{2,1,0:T(8,128)}, f32[32,64,256]{2,1,0:T(8,128)}, f32[32,64,256]{2,1,0:T(8,128)}, f32[32,64,256]{2,1,0:T(8,128)})) conditional(s32[]{:T(128)} %convert_element_type.3, (f32[256,128]{1,0:T(8,128)}, f32[32,64,256]{2,1,0:T(8,128)}, f32[32,64,256]{2,1,0:T(8,128)}, f32[32,64,256]{2,1,0:T(8,128)}, f32[32,64,256]{2,1,0:T(8,128)}, ...), branch_computations={%region_1.0_spmd, %region_2.0_spmd} | conditional | flops 393216 | bytes 3145736 | solution.py:840
  38.8 35.2 %branch_0_fun.1 = (f32[32,64,256]{2,1,0:T(8,128)}, f32[32,64,256]{2,1,0:T(8,128)}, f32[32,64,256]{2,1,0:T(8,128)}, f32[32,64,256]{2,1,0:T(8,128)}) custom-call(f32[256,128]{1,0:T(8,128)} %get-tuple-element.60.refs_0_, f32[32,64,256]{2,1,0:T(8,128)} %get-tuple-element.61.refs_1_, f32[32,64,256]{2,1,0:T(8,128)} %get-tuple-element.62.refs_2_, ...), custom_call_target="tpu_custom_call" | custom-call | tf_op jit(solution)/shard_map/cond/branch_0_fun/pallas_call | solution.py:759
Async XLA Ops:
  5.3 23.0 %collective-permute-start = (f32[14,64,256]{2,1,0:T(8,128)}, f32[14,64,256]{2,1,0:T(8,128)}, u32[]{:S(2)}, u32[]{:S(2)}) collective-permute-start(f32[14,64,256]{2,1,0:T(8,128)} %get-tuple-element.100), channel_id=1, source_target_pairs={{0,1},{1,0},{2,3},{3,2},{4,5},{5,4},{6,7},{7,6},{8,9},{9,8},{10,11... | collective-permute-start | bytes 2752520 | tf_op jit(solution)/shard_map/ppermute | solution.py:811
  5.9 22.5 %collective-permute-start.1 = (f32[14,64,256]{2,1,0:T(8,128)}, f32[14,64,256]{2,1,0:T(8,128)}, u32[]{:S(2)}, u32[]{:S(2)}) collective-permute-start(f32[14,64,256]{2,1,0:T(8,128)} %get-tuple-element.101), channel_id=1, source_target_pairs={{0,0},{1,2},{2,1},{3,4},{4,3},{5,6},{6,5},{7,7},{8,8},{9,10},{10,9... | collective-permute-start | bytes 2752520 | tf_op jit(solution)/shard_map/ppermute | solution.py:812
  14.2 24.6 %collective-permute-start.3 = (f32[416,256]{1,0:T(8,128)}, f32[416,256]{1,0:T(8,128)}, u32[]{:S(2)}, u32[]{:S(2)}) collective-permute-start(f32[416,256]{1,0:T(8,128)} %get-tuple-element.103.high_cols), channel_id=1, source_target_pairs={{0,8},{8,16},{16,24},{24,0},{1,9},{9,17},{17,25},{25,1},{2,10},{10... | collective-permute-start | bytes 1277960 | tf_op jit(solution)/shard_map/ppermute | solution.py:31
  16.7 22.1 %collective-permute-start.2 = (f32[384,256]{1,0:T(8,128)}, f32[384,256]{1,0:T(8,128)}, u32[]{:S(2)}, u32[]{:S(2)}) collective-permute-start(f32[384,256]{1,0:T(8,128)} %get-tuple-element.102.low_cols), channel_id=1, source_target_pairs={{0,24},{8,0},{16,8},{24,16},{1,25},{9,1},{17,9},{25,17},{2,26},{10... | collective-permute-start | bytes 1179656 | tf_op jit(solution)/shard_map/ppermute | solution.py:31
  23.3 13.2 %all-to-all-start.4 = ((f32[32,8,128]{2,1,0:T(8,128)}), f32[32,8,128]{2,1,0:T(8,128)}, u32[]{:S(2)}, u32[]{:S(2)}) async-start(f32[32,8,128]{2,1,0:T(8,128)} %bitcast.15), calls=%async_computation.4 | async-start | bytes 262144 | tf_op jit(solution)/shard_map/all_to_all | solution.py:822
  30.3 8.5 %collective-permute-start.4 = (f32[48,256]{1,0:T(8,128)}, f32[48,256]{1,0:T(8,128)}, u32[]{:S(2)}, u32[]{:S(2)}) collective-permute-start(f32[48,256]{1,0:T(8,128)} %get-tuple-element.104), channel_id=1, source_target_pairs={{0,24},{8,0},{16,8},{24,16},{1,25},{9,1},{17,9},{25,17},{2,26},{10... | collective-permute-start | bytes 147464 | tf_op jit(solution)/shard_map/ppermute | solution.py:31
  32.9 5.9 %collective-permute-start.5 = (f32[48,256]{1,0:T(8,128)}, f32[48,256]{1,0:T(8,128)}, u32[]{:S(2)}, u32[]{:S(2)}) collective-permute-start(f32[48,256]{1,0:T(8,128)} %get-tuple-element.105), channel_id=1, source_target_pairs={{0,8},{8,16},{16,24},{24,0},{1,9},{9,17},{17,25},{25,1},{2,10},{10... | collective-permute-start | bytes 147464 | tf_op jit(solution)/shard_map/ppermute | solution.py:31
